TPU v7x, 128 devices: a whole 4x4x4 slice. The times are simulated.
128 devices in a mesh: src: 32 (over x, z, core), tgt: 4 (over y).
Axes of the slice: x: 4, y: 4, z: 4, core: 2. Of those that a mesh axis runs over, the one named last changes fastest.
Arguments:
- source_embed: bfloat16 [16384, 768], P('src'), may hold values from -16 to 16
- target_embed: bfloat16 [8192, 768], P(('tgt', 'src')), may hold values from -6 to 6
- source_mass: float32 [16384], P('src'), may hold values from 0.3 to 3
- target_mass: float32 [8192], P('tgt'), may hold values from 0.3 to 3
Outputs:
- readout: float32 [16384, 768], P('src')
- source_potential: float32 [16384], P('src')
- target_potential: float32 [8192], P('tgt')
All inputs are finite; a program needn't handle non-finite values.
Results may differ from a plain program's by a relative error of at most 0.0028.
Values may be sent and summed in bfloat16 or wider, within the bound.
A program may use at most 64 MiB of HBM per device.

v0:
```python
import math

import jax
import jax.numpy as jnp
from jax import lax
from jax.sharding import PartitionSpec as P

D = 768
ITERS = 3


def block_scores(sources, block, scale):
    return (
        lax.dot_general(
            sources, block, (((1,), (1,)), ((), ())), preferred_element_type=jnp.float32
        )
        * scale
    )


def row_pass(sources, tgt_blocks, potential_g, scale):
    rows = sources.shape[0]

    def advance(carry, items):
        block, shift = items
        scores = block_scores(sources, block, scale) + shift[None, :]
        peak = jnp.maximum(carry[0], jnp.max(scores, axis=1))
        total = carry[1] * jnp.exp(carry[0] - peak) + jnp.sum(
            jnp.exp(scores - peak[:, None]), axis=1
        )
        return ((peak, total), None)

    start = (jnp.full((rows,), -1e30, jnp.float32), jnp.zeros((rows,), jnp.float32))
    return lax.scan(advance, start, (tgt_blocks, potential_g))[0]


def column_pass(sources, tgt_blocks, potential_f, scale):

    def single(block):
        scores = block_scores(sources, block, scale) + potential_f[:, None]
        peak = jnp.max(scores, axis=0)
        return (peak, jnp.sum(jnp.exp(scores - peak[None, :]), axis=0))

    return lax.map(single, tgt_blocks)


def shards(source_embed, target_embed, source_mass, target_mass):
    scale = 2.0 / math.sqrt(D)
    gathered = lax.all_gather(target_embed, "src", axis=0, tiled=True)
    total_rows = gathered.shape[0]
    width = 512
    count = total_rows // width
    tgt_blocks = gathered.reshape(count, width, gathered.shape[1])
    log_a = jnp.log(source_mass)
    log_b = jnp.log(target_mass).reshape(count, width)
    potential_g = jnp.zeros((count, width), jnp.float32)
    potential_f = jnp.zeros(log_a.shape, jnp.float32)
    for step in range(ITERS):
        peak, total = row_pass(source_embed, tgt_blocks, potential_g, scale)
        highest = lax.pmax(peak, "tgt")
        total = lax.psum(total * jnp.exp(peak - highest), "tgt")
        peak = highest
        potential_f = log_a - (peak + jnp.log(total))
        column_peak, column_total = column_pass(source_embed, tgt_blocks, potential_f, scale)
        column_high = lax.pmax(column_peak, "src")
        column_total = lax.psum(column_total * jnp.exp(column_peak - column_high), "src")
        column_peak = column_high
        potential_g = log_b - (column_peak + jnp.log(column_total))
    offset = potential_f - log_a

    def gather_step(carry, items):
        block, shift = items
        weights = jnp.exp(
            block_scores(source_embed, block, scale) + shift[None, :] + offset[:, None]
        )
        numer = carry[0] + jnp.dot(
            weights.astype(jnp.bfloat16), block, preferred_element_type=jnp.float32
        )
        return ((numer, carry[1] + jnp.sum(weights, axis=1)), None)

    rows = source_embed.shape[0]
    start = (jnp.zeros((rows, gathered.shape[1]), jnp.float32), jnp.zeros((rows,), jnp.float32))
    numerator, mass = lax.scan(gather_step, start, (tgt_blocks, potential_g))[0]
    numerator, mass = lax.psum((numerator, mass), "tgt")
    readout = numerator / mass[:, None]
    return (readout, potential_f, potential_g.reshape(total_rows))


def solution(mesh):
    placed = (P("src", None), P(("tgt", "src"), None), P("src"), P("tgt"))
    return jax.shard_map(
        shards,
        mesh=mesh,
        in_specs=placed,
        out_specs=(P("src", None), P("src"), P("tgt")),
        check_vma=False,
    )
```

profile of v0, /device:TPU:1, one launch (start us, length us, event | category | flops | bytes accessed | tf_op | source)
XLA Modules:
  0.0 622.1 jit_solution(17024977472537300388)
XLA Ops:
  7.2 0.7 all-gather.2.cloned.1.call-update
  8.0 0.7 log.24
  8.7 50.4 %all-gather.2.cloned.1.call-done = bf16[2048,768]{1,0:T(8,128)(2,1)} async-done(((bf16[64,768]{1,0:T(8,128)(2,1)}), bf16[2048,768]{1,0:T(8,128)(2,1)}) %all-gather.2.cloned.1.call-update) | async-done | bytes 3145744 | tf_op jit(solution)/shard_map/all_gather | solution.py:49
  59.1 9.0 %while.91 = (s32[]{:T(128)}, f32[512]{0:T(512)S(1)}, f32[512]{0:T(512)S(1)}, bf16[4,512,768]{2,1,0:T(8,128)(2,1)}, bf16[512,768]{1,0:T(8,128)(2,1)}, /*index=5*/s32[]{:T(128)}, s32[]{:T(128)}) while((s32[]{:T(128)}, f32[512]{0:T(512)S(1)}, f32[512]{0:T(512)S(1)}, bf16[4,512,768]{2,1,0:T(8,128)(2,1)}, bf16[512,768]{1,0:T(8,128)(2,1)}, ...), condition=%wide.region_3.4_spmd.clone, body=%wide.region_0.3_spmd.clone.sunk | while | flops 403704320 | bytes 3697240 | solution.py:34
  59.1 2.0 fusion.77
  61.1 0.2 exponential_reduce_fusion.15
  61.4 2.0 fusion.77
  63.6 2.0 fusion.77
  65.6 0.2 exponential_reduce_fusion.15
  65.8 2.0 fusion.77
  67.9 0.2 exponential_reduce_fusion.15
  68.1 8.5 %pmax.42 = f32[512]{0:T(512)S(1)} all-reduce(f32[512]{0:T(512)S(1)} %get-tuple-element.234), channel_id=1, replica_groups=mesh['src'=32,'tgt'=4] {'tgt'}, use_global_device_ids=true, to_apply=%region_4.5 | all-reduce | flops 512 | bytes 4096 | tf_op jit(solution)/shard_map/pmax | solution.py:60
  76.5 6.0 psum.56
  82.6 9.2 %while.88 = (s32[]{:T(128)}, f32[4,512]{1,0:T(4,128)S(1)}, f32[4,512]{1,0:T(4,128)S(1)}, bf16[4,512,768]{2,1,0:T(8,128)(2,1)}, bf16[512,768]{1,0:T(8,128)(2,1)}, /*index=5*/f32[512]{0:T(512)S(1)}, s32[]{:T(128)}, s32[]{:T(128)}) while((s32[]{:T(128)}, f32[4,512]{1,0:T(4,128)S(1)}, f32[4,512]{1,0:T(4,128)S(1)}, ...), condition=%wide.region_9.10_spmd, body=%wide.region_6.9_spmd.sunk | while | flops 403962880 | bytes 3687005 | solution.py:44
  82.6 2.0 fusion.71
  84.6 0.2 exponential_reduce_fusion.12
  84.9 2.0 fusion.71
  86.9 0.2 exponential_reduce_fusion.12
  87.2 2.0 fusion.71
  89.5 2.0 fusion.71
  91.8 67.0 %pmax.43 = f32[4,512]{1,0:T(4,128)S(1)} all-reduce(f32[4,512]{1,0:T(4,128)S(1)} %get-tuple-element.236), channel_id=1, replica_groups=mesh['src'=32,'tgt'=4] {'src'}, use_global_device_ids=true, to_apply=%region_10.11 | all-reduce | flops 2048 | bytes 16384 | tf_op jit(solution)/shard_map/pmax | solution.py:65
  158.8 63.7 %psum.57 = f32[4,512]{1,0:T(4,128)S(1)} all-reduce(f32[4,512]{1,0:T(4,128)S(1)} %exponential_multiply_fusion.2), channel_id=1, replica_groups=mesh['src'=32,'tgt'=4] {'src'}, use_global_device_ids=true, to_apply=%region_11.12 | all-reduce | flops 2048 | bytes 16384 | tf_op jit(solution)/shard_map/psum | solution.py:66
  222.6 9.0 %while.92 = (s32[]{:T(128)}, f32[512]{0:T(512)S(1)}, f32[512]{0:T(512)S(1)}, bf16[4,512,768]{2,1,0:T(8,128)(2,1)}, bf16[512,768]{1,0:T(8,128)(2,1)}, /*index=5*/f32[4,512]{1,0:T(4,128)S(1)}, s32[]{:T(128)}, s32[]{:T(128)}) while((s32[]{:T(128)}, f32[512]{0:T(512)S(1)}, f32[512]{0:T(512)S(1)}, bf16[4,512,768]{2,1,0:T(8,128)(2,1)}, ...), condition=%wide.region_15.16_spmd.clone, body=%wide.region_12.15_spmd.clone.sunk | while | flops 403966464 | bytes 3703396 | solution.py:34
  222.6 2.0 fusion.80
  224.9 2.0 fusion.80
  227.1 2.0 fusion.80
  229.4 2.0 fusion.80
  231.6 7.7 %pmax.44 = f32[512]{0:T(512)S(1)} all-reduce(f32[512]{0:T(512)S(1)} %get-tuple-element.238), channel_id=1, replica_groups=mesh['src'=32,'tgt'=4] {'tgt'}, use_global_device_ids=true, to_apply=%region_16.17 | all-reduce | flops 512 | bytes 4096 | tf_op jit(solution)/shard_map/pmax | solution.py:60
  239.3 6.0 psum.58
  245.4 9.2 %while.89 = (s32[]{:T(128)}, f32[4,512]{1,0:T(4,128)S(1)}, f32[4,512]{1,0:T(4,128)S(1)}, bf16[4,512,768]{2,1,0:T(8,128)(2,1)}, bf16[512,768]{1,0:T(8,128)(2,1)}, /*index=5*/f32[512]{0:T(512)S(1)}, s32[]{:T(128)}, s32[]{:T(128)}) while((s32[]{:T(128)}, f32[4,512]{1,0:T(4,128)S(1)}, f32[4,512]{1,0:T(4,128)S(1)}, ...), condition=%wide.region_21.22_spmd, body=%wide.region_18.21_spmd.sunk | while | flops 403962880 | bytes 3687005 | solution.py:44
  245.4 2.0 fusion.73
  247.7 2.0 fusion.73
  250.0 2.0 fusion.73
  252.3 2.0 fusion.73
  254.6 67.4 %pmax.45 = f32[4,512]{1,0:T(4,128)S(1)} all-reduce(f32[4,512]{1,0:T(4,128)S(1)} %get-tuple-element.240), channel_id=1, replica_groups=mesh['src'=32,'tgt'=4] {'src'}, use_global_device_ids=true, to_apply=%region_22.23 | all-reduce | flops 2048 | bytes 16384 | tf_op jit(solution)/shard_map/pmax | solution.py:65
  322.1 63.7 %psum.59 = f32[4,512]{1,0:T(4,128)S(1)} all-reduce(f32[4,512]{1,0:T(4,128)S(1)} %exponential_multiply_fusion.1), channel_id=1, replica_groups=mesh['src'=32,'tgt'=4] {'src'}, use_global_device_ids=true, to_apply=%region_23.24 | all-reduce | flops 2048 | bytes 16384 | tf_op jit(solution)/shard_map/psum | solution.py:66
  385.8 9.0 %while.93 = (s32[]{:T(128)}, f32[512]{0:T(512)S(1)}, f32[512]{0:T(512)S(1)}, bf16[4,512,768]{2,1,0:T(8,128)(2,1)}, bf16[512,768]{1,0:T(8,128)(2,1)}, /*index=5*/f32[4,512]{1,0:T(4,128)S(1)}, s32[]{:T(128)}, s32[]{:T(128)}) while((s32[]{:T(128)}, f32[512]{0:T(512)S(1)}, f32[512]{0:T(512)S(1)}, bf16[4,512,768]{2,1,0:T(8,128)(2,1)}, ...), condition=%wide.region_27.28_spmd.clone, body=%wide.region_24.27_spmd.clone.sunk | while | flops 403966464 | bytes 3703396 | solution.py:34
  385.8 2.0 fusion.83
  388.1 2.0 fusion.83
  390.3 2.0 fusion.83
  392.6 2.0 fusion.83
  394.8 7.7 %pmax.46 = f32[512]{0:T(512)S(1)} all-reduce(f32[512]{0:T(512)S(1)} %get-tuple-element.242), channel_id=1, replica_groups=mesh['src'=32,'tgt'=4] {'tgt'}, use_global_device_ids=true, to_apply=%region_28.29 | all-reduce | flops 512 | bytes 4096 | tf_op jit(solution)/shard_map/pmax | solution.py:60
  402.6 6.0 psum.60
  408.6 9.2 %while.90 = (s32[]{:T(128)}, f32[4,512]{1,0:T(4,128)S(1)}, f32[4,512]{1,0:T(4,128)S(1)}, bf16[4,512,768]{2,1,0:T(8,128)(2,1)}, bf16[512,768]{1,0:T(8,128)(2,1)}, /*index=5*/f32[512]{0:T(512)S(1)}, s32[]{:T(128)}, s32[]{:T(128)}) while((s32[]{:T(128)}, f32[4,512]{1,0:T(4,128)S(1)}, f32[4,512]{1,0:T(4,128)S(1)}, ...), condition=%wide.region_33.34_spmd, body=%wide.region_30.33_spmd.sunk | while | flops 403962880 | bytes 3687005 | solution.py:44
  408.6 2.0 fusion.75
  410.9 2.0 fusion.75
  413.2 2.0 fusion.75
  415.5 2.0 fusion.75
  417.9 67.4 %pmax.47 = f32[4,512]{1,0:T(4,128)S(1)} all-reduce(f32[4,512]{1,0:T(4,128)S(1)} %get-tuple-element.244), channel_id=1, replica_groups=mesh['src'=32,'tgt'=4] {'src'}, use_global_device_ids=true, to_apply=%region_34.35 | all-reduce | flops 2048 | bytes 16384 | tf_op jit(solution)/shard_map/pmax | solution.py:65
  485.3 63.7 %psum.61 = f32[4,512]{1,0:T(4,128)S(1)} all-reduce(f32[4,512]{1,0:T(4,128)S(1)} %exponential_multiply_fusion), channel_id=1, replica_groups=mesh['src'=32,'tgt'=4] {'src'}, use_global_device_ids=true, to_apply=%region_35.36 | all-reduce | flops 2048 | bytes 16384 | tf_op jit(solution)/shard_map/psum | solution.py:66
  549.1 16.6 %while.94 = (s32[]{:T(128)}, f32[512,768]{1,0:T(8,128)S(1)}, f32[512]{0:T(512)S(1)}, bf16[4,512,768]{2,1,0:T(8,128)(2,1)}, bf16[512,768]{1,0:T(8,128)(2,1)}, /*i...) while((s32[]{:T(128)}, f32[512,768]{1,0:T(8,128)S(1)}, f32[512]{0:T(512)S(1)}, ...), condition=%wide.region_38.39_spmd.clone, body=%wide.region_36.38_spmd.clone.sunk | while | flops 807404032 | bytes 6571116 | solution.py:83
  549.1 2.1 fusion.88
  551.2 2.0 select_add_fusion.4
  553.2 2.1 fusion.88
  555.3 2.0 select_add_fusion.4
  557.4 2.1 fusion.88
  559.5 2.0 select_add_fusion.4
  561.5 2.1 fusion.88
  563.6 2.0 select_add_fusion.4
  565.6 1.1 copy-done
  566.8 0.6 copy.7
  567.4 8.6 %psum.63 = f32[512]{0:T(512)S(1)} all-reduce(f32[512]{0:T(512)S(1)} %get-tuple-element.247), channel_id=1, replica_groups=mesh['src'=32,'tgt'=4] {'tgt'}, use_global_device_ids=true, to_apply=%region_40.41 | all-reduce | flops 512 | bytes 4096 | tf_op jit(solution)/shard_map/psum | solution.py:84
  576.0 36.6 %all-reduce.2.cloned.1.call-done = f32[512,768]{1,0:T(8,128)} async-done(((f32[512,768]{1,0:T(8,128)}), f32[512,768]{1,0:T(8,128)}) %all-reduce.2.cloned.1.call-update) | async-done | bytes 1572880 | tf_op jit(solution)/shard_map/psum | solution.py:84
  612.6 2.7 broadcast_divide_fusion
  (130 shorter events, 5.5 us)
Async XLA Ops:
  7.2 51.9 %all-gather.2.cloned.1.call-start = ((), (), s32[]{:S(2)}) async-start(), calls=%async_computation | async-start | bytes 3244032 | tf_op jit(solution)/shard_map/all_gather | solution.py:49
  7.9 604.7 %all-reduce.2.cloned.1.call-start = ((), (), s32[]{:S(2)}) async-start(), calls=%async_computation.1 | async-start | bytes 3145728 | tf_op jit(solution)/shard_map/psum | solution.py:84
  59.1 23.4 %copy-start.1 = (f32[512]{0:T(512)S(1)}, f32[512]{0:T(512)}, u32[]{:S(2)}) copy-start(f32[512]{0:T(512)} %param.20) | copy-start | bytes 6148
  417.9 131.2 %copy-start.2 = (f32[512]{0:T(512)}, f32[512]{0:T(512)S(1)}, u32[]{:S(2)}) copy-start(f32[512]{0:T(512)S(1)} %get-tuple-element.904) | copy-start | bytes 6148
  565.6 1.1 copy-start
Sparse Core Ops, SparseCore 0:
  10.3 48.8 all-gather.1
  566.9 45.5 all-reduce.1
where the time goes:
time: 623 us; the launch traced here: 622 us
  blocking collectives  443 us (71%)
  waiting for transfers between devices  87.7 us (14%)
  matrix products  64.1 us (10%)
  between operations  14.3 us (2%)
  other arithmetic  7.88 us (1%)
    pmax x3, blocking collectives, shards(): column_high = lax.pmax(column_peak, 'src')  202 us
    psum x3, blocking collectives, shards(): lax.psum(column_total * jnp.exp(column_peak - column_high), 'src')  191 us
    dot_general x28, matrix products, block_scores(): lax.dot_general(sources, block, (((1,), (1,)), ((), ())), preferred_eleme...  56.1 us
    all_gather x1, waiting for transfers between devices, shards(): gathered = lax.all_gather(target_embed, 'src', axis=0, tiled=True)  50.4 us
    psum x1, waiting for transfers between devices, shards(): numerator, mass = lax.psum((numerator, mass), 'tgt')  36.6 us
    pmax x3, blocking collectives, shards(): highest = lax.pmax(peak, 'tgt')  23.9 us
    psum x3, blocking collectives, shards(): total = lax.psum(total * jnp.exp(peak - highest), 'tgt')  18 us
  transfers between devices with their start and end apart: 2, of which 2 were waited for; matrix products, arithmetic and copies ran while one was open for 0% of the time, Pallas kernels for 0%

commit v1 on v0

v1 whole, which is shorter than its diff:
```python
import functools
import math

import jax
import jax.numpy as jnp
from jax import lax
from jax.experimental import pallas as pl
from jax.experimental.pallas import tpu as pltpu
from jax.sharding import PartitionSpec as P

D = 768
HALF = D // 2
ITERS = 3
MESH = pl.DeviceIdType.MESH
SCALE = 2.0 / math.sqrt(D) * math.log2(math.e)
LN2 = math.log(2.0)
NT = (((1,), (1,)), ((), ()))
F32 = jnp.float32


def place():
    s = lax.axis_index("src")
    return s // 8, lax.axis_index("tgt"), (s // 2) % 4, s % 2


def device(x, y, z, c):
    return ((x * 4 + z) * 2 + c, y)


def row_peers(at):
    x, y, z, c = at
    peers = [
        (x, (y + step) % 4, z, (c + other) % 2) for step in (2, 1, 3) for other in (1, 0)
    ]
    return peers + [(x, y, z, 1 - c)]


def column_peers(at):
    x, y, z, c = at
    steps = [(a, b) for a in range(4) for b in range(4) if a or b]
    steps.sort(key=lambda t: -(min(t[0], 4 - t[0]) + min(t[1], 4 - t[1])))
    return [((x + a) % 4, y, (z + b) % 4, c) for a, b in steps]


def remote(src, dst, send, recv, to):
    return pltpu.make_async_remote_copy(
        src_ref=src,
        dst_ref=dst,
        send_sem=send,
        recv_sem=recv,
        device_id=device(*to),
        device_id_type=MESH,
    )


def gather_steps(targets, at, planes, send, recv, started):
    x, y, z, c = at
    copies = {}

    def go(h, k, first, second, low, rows, axis, step):
        a, b = (first, second) if h == 0 else (second, first)
        row = pl.multiple_of(((x + a) % 4 * 4 + (z + b) % 4) * 64 + low, 32)
        block = targets.at[c, planes, pl.ds(row, rows), pl.ds(h * HALF, HALF)]
        along_x = (axis == 1) == (h == 0)
        to = ((x + step) % 4, y, z, c) if along_x else (x, y, (z + step) % 4, c)
        copy = remote(block, block, send.at[h, k], recv.at[h, k], to)
        copy.start()
        copies[h, k] = copy
        started.append(copy)

    def second_axis(h, b, first):
        go(h, 4 + 4 * b, first, 0, 0, 64, 2, 1)
        go(h, 5 + 4 * b, first, 0, 0, 64, 2, -1)

    def forward(h, b, first):
        copies[h, 4 + 4 * b].wait_recv()
        go(h, 6 + 4 * b, first, -1, 0, 32, 2, 1)
        copies[h, 5 + 4 * b].wait_recv()
        go(h, 7 + 4 * b, first, 1, 32, 32, 2, -1)

    both = (0, 1)
    for h in both:
        go(h, 0, 0, 0, 0, 64, 1, 1)
        go(h, 1, 0, 0, 0, 64, 1, -1)
    for h in both:
        second_axis(h, 0, 0)
    yield
    for h in both:
        copies[h, 0].wait_recv()
        go(h, 2, -1, 0, 0, 32, 1, 1)
        second_axis(h, 1, -1)
        copies[h, 1].wait_recv()
        go(h, 3, 1, 0, 32, 32, 1, -1)
        second_axis(h, 2, 1)
    yield
    for h in both:
        forward(h, 0, 0)
    for h in both:
        copies[h, 2].wait_recv()
        copies[h, 3].wait_recv()
        second_axis(h, 3, 2)
    yield
    for b, first in ((1, -1), (2, 1)):
        for h in both:
            forward(h, b, first)
    yield
    for h in both:
        forward(h, 3, 2)
    yield
    for b in range(4):
        for h in both:
            copies[h, 6 + 4 * b].wait_recv()
            copies[h, 7 + 4 * b].wait_recv()


def combine(parts):
    peak = functools.reduce(jnp.maximum, parts)
    return peak + jnp.log2(functools.reduce(jnp.add, [jnp.exp2(p - peak) for p in parts]))


def row_pass(scores, g, out):
    lane = lax.broadcasted_iota(jnp.int32, (8, 128), 1)
    sub = lax.broadcasted_iota(jnp.int32, (8, 128), 0)
    shifts = [jnp.broadcast_to(g[k : k + 1, :], (8, 128)) for k in range(8)]

    def block(q, _):
        def group(i, acc):
            r = pl.multiple_of(q * 128 + i * 8, 8)
            xs = [scores[pl.ds(r, 8), pl.ds(128 * k, 128)] + shifts[k] for k in range(8)]
            peak = jnp.max(functools.reduce(jnp.maximum, xs), axis=1, keepdims=True)
            total = functools.reduce(jnp.add, [jnp.exp2(x - peak) for x in xs])
            value = peak + jnp.log2(jnp.sum(total, axis=1, keepdims=True))
            return jnp.where(lane - i * 8 == sub, value, acc)

        acc = lax.fori_loop(0, 16, group, jnp.zeros((8, 128), F32), unroll=16)
        out[pl.ds(q, 1), :] = jnp.sum(acc, axis=0, keepdims=True)
        return 0

    lax.fori_loop(0, 8, block, 0, unroll=2)


def spread(values, out):
    for q in range(values.shape[0]):
        out[pl.ds(q * 128, 128), :] = jnp.broadcast_to(values[q : q + 1, :], (128, 128)).T


def column_pass(scores, f_rows, out):
    def peaks(i, carry):
        r = pl.multiple_of(i * 8, 8)
        f = f_rows[pl.ds(r, 8), :]
        return tuple(
            jnp.maximum(carry[k], scores[pl.ds(r, 8), pl.ds(128 * k, 128)] + f)
            for k in range(8)
        )

    start = tuple(jnp.full((8, 128), -1e30, F32) for _ in range(8))
    top = lax.fori_loop(0, 128, peaks, start, unroll=16)
    top = [jnp.broadcast_to(jnp.max(t, axis=0, keepdims=True), (8, 128)) for t in top]

    def sums(i, carry):
        r = pl.multiple_of(i * 8, 8)
        f = f_rows[pl.ds(r, 8), :]
        return tuple(
            carry[k] + jnp.exp2(scores[pl.ds(r, 8), pl.ds(128 * k, 128)] + f - top[k])
            for k in range(8)
        )

    start = tuple(jnp.zeros((8, 128), F32) for _ in range(8))
    total = lax.fori_loop(0, 128, sums, start, unroll=16)
    for k in range(8):
        out[k : k + 1, :] = top[k][0:1] + jnp.log2(jnp.sum(total[k], axis=0, keepdims=True))


def kernel(
    source_ref, target_ref, a_ref, b_ref, readout_ref, f_ref, g_ref,
    sources, targets, masses, scores, wide, f_rows, mass_rows, row_buf, column_buf, g_buf,
    own_send, own_recv, far_send, far_recv, y_send, y_recv, in_send, in_recv,
    row_send, row_recv, column_send, column_recv, g_send, g_recv, core_send, core_recv,
):
    at = place()
    x, y, z, c = at
    rows, columns = row_peers(at), column_peers(at)
    barrier = pltpu.get_barrier_semaphore()
    for peer in columns + rows:
        pl.semaphore_signal(barrier, inc=1, device_id=device(*peer), device_id_type=MESH)
    pl.semaphore_wait(barrier, len(columns) + len(rows))

    sibling = (x, y, z, 1 - c)
    started = []
    own_rows = pl.ds(pl.multiple_of((x * 4 + z) * 64, 64), 64)
    half_rows = pl.ds(pl.multiple_of(c * 512, 512), 512)
    targets[c, 0, own_rows, :] = target_ref[...]
    sources[half_rows, :] = source_ref[...]
    masses[c] = a_ref[...]

    own = gather_steps(targets, at, pl.ds(0, 1), own_send, own_recv, started)
    next(own)
    crossings = []
    for k, step in enumerate((1, 3, 2)):
        dst = targets.at[c, 4 - step, own_rows]
        copy = remote(target_ref, dst, y_send.at[k], y_recv.at[k], (x, (y + step) % 4, z, c))
        copy.start()
        crossings.append(copy)
    inner = [
        remote(source_ref, sources.at[half_rows], in_send.at[0], in_recv.at[0], sibling),
        remote(a_ref, masses.at[c], in_send.at[1], in_recv.at[1], sibling),
    ]
    for copy in inner:
        copy.start()
    started += crossings + inner
    for _ in own:
        pass
    for copy in crossings:
        copy.wait_recv()
    far = gather_steps(targets, at, pl.ds(1, 3), far_send, far_recv, started)
    for _ in far:
        pass

    for copy in inner:
        copy.wait_recv()
    passed = []
    for k in range(8):
        part = targets.at[c, k // 2, pl.ds(k % 2 * 512, 512)]
        copy = remote(part, part, core_send.at[k], core_recv.at[k], sibling)
        copy.start()
        passed.append(copy)
    started += passed

    log_a = jnp.log2(jnp.concatenate([masses[0], masses[1]], axis=0))
    left = lax.broadcasted_iota(jnp.int32, (8, 128), 1) < 64
    even, odd = b_ref[pl.ds(0, 8, stride=2), :], b_ref[pl.ds(1, 8, stride=2), :]
    log_b = jnp.log2(
        jnp.where(
            c == 0,
            jnp.where(left, even, pltpu.roll(odd, 64, 1)),
            jnp.where(left, pltpu.roll(even, 64, 1), odd),
        )
    )

    for k in range(4):
        scores[:, k * 256 : (k + 1) * 256] = (
            lax.dot_general(
                sources[...],
                targets[c, 0, k * 256 : (k + 1) * 256, :],
                NT,
                preferred_element_type=F32,
            )
            * SCALE
        )

    def exchange(buf, me, peers, send, recv):
        for peer in peers:
            remote(buf.at[me], buf.at[me], send, recv, peer).start()

    def drain(buf, peers, sem):
        every = buf.at[pl.ds(0, len(peers))]
        pltpu.make_async_copy(every, every, sem).wait()

    g = jnp.zeros((8, 128), F32)
    row_me, column_me = y * 2 + c, x * 4 + z
    for it in range(ITERS):
        row_pass(scores, g, row_buf.at[it, row_me])
        exchange(row_buf.at[it], row_me, rows, row_send.at[it], row_recv.at[it])
        drain(row_buf.at[it], rows, row_recv.at[it])
        lse = combine([row_buf[it, k] for k in range(8)])
        f = log_a - lse
        spread(f, f_rows)
        column_pass(scores, f_rows, column_buf.at[it, column_me])
        exchange(column_buf.at[it], column_me, columns, column_send.at[it], column_recv.at[it])
        drain(column_buf.at[it], columns, column_recv.at[it])
        g = log_b - combine([column_buf[it, k] for k in range(16)])

    g_buf[c, 0] = g
    for other in (1, 0):
        for step in (2, 1, 3, 0):
            if step or other:
                to = (x, (y + step) % 4, z, (c + other) % 2)
                dst = g_buf.at[c, (4 - step) % 4]
                remote(g_buf.at[c, 0], dst, g_send, g_recv, to).start()
    every = row_buf.at[0, pl.ds(0, 7)]
    pltpu.make_async_copy(every, every, g_recv).wait()
    for copy in passed:
        copy.wait_recv()

    f_ref[...] = jnp.where(c == 0, f[0:4], f[4:8]) * LN2
    g0, g1 = g_buf[0, 0] * LN2, g_buf[1, 0] * LN2
    g_ref[pl.ds(0, 8, stride=2), :] = jnp.where(left, g0, pltpu.roll(g1, 64, 1))
    g_ref[pl.ds(1, 8, stride=2), :] = jnp.where(left, pltpu.roll(g0, 64, 1), g1)

    spread(jnp.where(c == 0, -lse[0:4], -lse[4:8]), f_rows)
    for k in range(8):
        wide[k] = (
            lax.dot_general(
                source_ref[...], targets[k // 4, k % 4], NT, preferred_element_type=F32
            )
            * SCALE
        )
    readout_ref[...] = jnp.zeros_like(readout_ref)
    mass_rows[...] = jnp.zeros_like(mass_rows)

    def part(k, _):
        base = f_rows[0:512, :]
        mass = mass_rows[...]
        weights = []
        for q in range(8):
            shift = g_buf[k // 4, k % 4, q : q + 1, :]
            w = jnp.exp2(wide[k, :, pl.ds(q * 128, 128)] + base + shift)
            mass = mass + w
            weights.append(w)
        mass_rows[...] = mass
        low = jnp.concatenate(weights, axis=1).astype(jnp.bfloat16)
        readout_ref[...] += jnp.dot(low, targets[k // 4, k % 4], preferred_element_type=F32)
        return 0

    lax.fori_loop(0, 8, part, 0)
    readout_ref[...] = readout_ref[...] / jnp.sum(mass_rows[...], axis=1, keepdims=True)

    for copy in started:
        copy.wait_send()
    for it in range(ITERS):
        drain(row_buf.at[it], rows, row_send.at[it])
        drain(column_buf.at[it], columns, column_send.at[it])
    pltpu.make_async_copy(every, every, g_send).wait()


def shards(source_embed, target_embed, source_mass, target_mass):
    vmem, dma = pltpu.VMEM, pltpu.SemaphoreType.DMA
    bf16 = jnp.bfloat16
    readout, f, g = pl.pallas_call(
        kernel,
        out_shape=(
            jax.ShapeDtypeStruct((512, D), F32),
            jax.ShapeDtypeStruct((4, 128), F32),
            jax.ShapeDtypeStruct((16, 128), F32),
        ),
        in_specs=[pl.BlockSpec(memory_space=vmem)] * 4,
        out_specs=(pl.BlockSpec(memory_space=vmem),) * 3,
        scratch_shapes=[
            vmem((1024, D), bf16),
            vmem((2, 4, 1024, D), bf16),
            vmem((2, 4, 128), F32),
            vmem((1024, 1024), F32),
            vmem((8, 512, 1024), F32),
            vmem((1024, 128), F32),
            vmem((512, 128), F32),
            vmem((ITERS, 8, 8, 128), F32),
            vmem((ITERS, 16, 8, 128), F32),
            vmem((2, 4, 8, 128), F32),
            dma((2, 20)),
            dma((2, 20)),
            dma((2, 20)),
            dma((2, 20)),
            dma((3,)),
            dma((3,)),
            dma((2,)),
            dma((2,)),
            dma((ITERS,)),
            dma((ITERS,)),
            dma((ITERS,)),
            dma((ITERS,)),
            dma(()),
            dma(()),
            dma((8,)),
            dma((8,)),
        ],
        name="sinkhorn",
        compiler_params=pltpu.CompilerParams(
            collective_id=0, has_side_effects=True, vmem_limit_bytes=56 << 20
        ),
    )(source_embed, target_embed, source_mass.reshape(4, 128), target_mass.reshape(16, 128))
    return readout, f.reshape(512), g.reshape(2048)


def solution(mesh):
    placed = (P("src", None), P(("tgt", "src"), None), P("src"), P("tgt"))
    return jax.shard_map(
        shards,
        mesh=mesh,
        in_specs=placed,
        out_specs=(P("src", None), P("src"), P("tgt")),
        check_vma=False,
    )
```

time: 623 us -> 114 us (0.18)
  blocking collectives: 443 us -> 0 us
  Pallas kernels: 0 us -> 109 us
  waiting for transfers between devices: 87.7 us -> 0 us
  matrix products: 64.1 us -> 0 us
  between operations: 14.3 us -> 0.66 us
  other arithmetic: 7.88 us -> 0 us
    pmax x6 -> x0, blocking collectives: 226 us -> none  [the longest x3 202 us: shards(): column_high = lax.pmax(column_peak, 'src')]
    psum x7 -> x0, blocking collectives: 218 us -> none  [the longest x3 191 us: shards(): lax.psum(column_total * jnp.exp(column_peak - column_high), 'src')]
    pallas_call x0 -> x1, Pallas kernels: none -> 109 us  [shards(): pl.pallas_call(kernel, out_shape=(jax.ShapeDtypeStruct((512, D), F32), ja...]
    dot_general x32 -> x0, matrix products: 64.1 us -> none  [the longest x28 56.1 us: block_scores(): lax.dot_general(sources, block, (((1,), (1,)), ((), ())), preferred_eleme...]
    all_gather x1 -> x0, waiting for transfers between devices: 50.4 us -> none  [shards(): gathered = lax.all_gather(target_embed, 'src', axis=0, tiled=True)]
    psum x1 -> x0, waiting for transfers between devices: 36.6 us -> none  [shards(): numerator, mass = lax.psum((numerator, mass), 'tgt')]
  transfers between devices with their start and end apart: 2 -> 0, of which waited for: 2 -> 0; matrix products, arithmetic and copies ran while one was open for 0% -> 0% of each run, Pallas kernels for 0% -> 0%
where the time goes in v1:
time: 114 us; the launch traced here: 113 us
  Pallas kernels  109 us (96%)
  local copies, waits for them, and re-layouts  3.84 us (3%)
    pallas_call x1, Pallas kernels, shards(): pl.pallas_call(kernel, out_shape=(jax.ShapeDtypeStruct((512, D), F32), ja...  109 us
    unnamed x7, local copies, waits for them, and re-layouts  3.84 us

profile of v1, /device:TPU:1, one launch (start us, length us, event | category | flops | bytes accessed | tf_op | source)
XLA Modules:
  0.0 113.5 jit_solution(11363342468602383067)
XLA Ops:
  0.6 109.0 %sinkhorn.1 = (f32[512,768]{1,0:T(8,128)}, f32[4,128]{1,0:T(4,128)}, f32[16,128]{1,0:T(8,128)}) custom-call(bf16[512,768]{1,0:T(8,128)(2,1)} %source_ref.1, bf16[64,768]{1,0:T(8,128)(2,1)} %target_ref.1, f32[4,128]{1,0:T(4,128)} %bitcast.6, f32[16,128]{1,0:T(8,128)} %bitcast.4), custom_call_target="tpu_custom_call" | custom-call | tf_op jit(solution)/shard_map/sinkhorn/pallas_call | solution.py:329
  109.6 0.0 copy-start.1
  109.6 0.0 copy-start
  109.7 2.7 %copy.10 = f32[512,768]{1,0:T(8,128)} copy(f32[512,768]{1,0:T(8,128)} %get-tuple-element.12) | data formatting | bytes 3145728
  112.3 0.0 copy-done.1
  112.3 0.6 copy.11
  112.9 0.0 copy-done
  112.9 0.6 copy.12
Async XLA Ops:
  109.6 2.7 %copy-start.1 = (f32[4,128]{1,0:T(4,128)S(1)}, f32[4,128]{1,0:T(4,128)}, u32[]{:S(2)}) copy-start(f32[4,128]{1,0:T(4,128)} %get-tuple-element.7) | copy-start | bytes 6148
  109.6 3.3 %copy-start = (f32[16,128]{1,0:T(8,128)S(1)}, f32[16,128]{1,0:T(8,128)}, u32[]{:S(2)}) copy-start(f32[16,128]{1,0:T(8,128)} %get-tuple-element.8) | copy-start | bytes 24580

commit v2 on v1

v2 whole, which is shorter than its diff:
```python
import functools
import math

import jax
import jax.numpy as jnp
from jax import lax
from jax.experimental import pallas as pl
from jax.experimental.pallas import tpu as pltpu
from jax.sharding import PartitionSpec as P

D = 768
ITERS = 3
MESH = pl.DeviceIdType.MESH
SCALE = 2.0 / math.sqrt(D) * math.log2(math.e)
LN2 = math.log(2.0)
NT = (((1,), (1,)), ((), ()))
F32 = jnp.float32


def place():
    s = lax.axis_index("src")
    return s // 8, lax.axis_index("tgt"), (s // 2) % 4, s % 2


def device(x, y, z, c):
    return ((x * 4 + z) * 2 + c, y)


def row_peers(at):
    x, y, z, c = at
    peers = [
        (x, (y + step) % 4, z, (c + other) % 2) for step in (2, 1, 3) for other in (1, 0)
    ]
    return peers + [(x, y, z, 1 - c)]


def column_peers(at):
    x, y, z, c = at
    steps = [(a, b) for a in range(4) for b in range(4) if a or b]
    steps.sort(key=lambda t: -(min(t[0], 4 - t[0]) + min(t[1], 4 - t[1])))
    return [((x + a) % 4, y, (z + b) % 4, c) for a, b in steps]


def remote(src, dst, send, recv, to):
    return pltpu.make_async_remote_copy(
        src_ref=src,
        dst_ref=dst,
        send_sem=send,
        recv_sem=recv,
        device_id=device(*to),
        device_id_type=MESH,
    )


class Gather:
    def __init__(self, targets, planes, at, send, recv):
        self.targets, self.planes = targets, planes
        self.x, self.y, self.z, self.c = at
        self.u = self.x * (1 - self.c) + self.z * self.c
        self.v = self.z * (1 - self.c) + self.x * self.c
        self.send, self.recv = send, recv
        self.copies = {}

    def shift(self, du, dv):
        x = (self.x + du * (1 - self.c) + dv * self.c) % 4
        z = (self.z + du * self.c + dv * (1 - self.c)) % 4
        return (x, self.y, z, self.c)

    def go(self, stage, k, du, dv, low, to):
        row = ((self.u + du) % 4 * 4 + (self.v + dv) % 4) * 64 + low
        block = self.targets.at[self.planes, pl.ds(pl.multiple_of(row, 32), 32), :]
        copy = remote(block, block, self.send.at[stage, k], self.recv.at[stage, k], to)
        copy.start()
        self.copies[stage, k] = copy

    def both_ways(self, stage, du, up, down):
        self.go(stage, 0, du, 0, 0, up)
        self.go(stage, 2, du, 0, 32, down)
        self.go(stage, 1, du, 0, 32, up)
        self.go(stage, 3, du, 0, 0, down)

    def first(self):
        self.both_ways(4, 0, self.shift(1, 0), self.shift(3, 0))

    def first_forward(self):
        self.copies[4, 0].wait_recv()
        self.go(4, 4, 3, 0, 0, self.shift(1, 0))
        self.copies[4, 2].wait_recv()
        self.go(4, 5, 1, 0, 32, self.shift(3, 0))

    def second(self, du):
        if du == 3:
            self.copies[4, 1].wait_recv()
        if du == 1:
            self.copies[4, 3].wait_recv()
        if du == 2:
            self.copies[4, 4].wait_recv()
            self.copies[4, 5].wait_recv()
        self.both_ways(du, du, self.shift(0, 1), self.shift(0, 3))

    def second_forward(self, du):
        self.copies[du, 0].wait_recv()
        self.go(du, 4, du, 3, 0, self.shift(0, 1))
        self.copies[du, 2].wait_recv()
        self.go(du, 5, du, 1, 32, self.shift(0, 3))

    def arrived(self, du):
        for k in (1, 3, 4, 5):
            self.copies[du, k].wait_recv()
        return pl.multiple_of((self.u + du) % 4 * 256, 256)

    def finish(self):
        for copy in self.copies.values():
            copy.wait_send()


def combine(parts):
    peak = functools.reduce(jnp.maximum, parts)
    return peak + jnp.log2(functools.reduce(jnp.add, [jnp.exp2(p - peak) for p in parts]))


def row_pass(scores, g, out, first=0, width=8):
    lane = lax.broadcasted_iota(jnp.int32, (8, 128), 1)
    sub = lax.broadcasted_iota(jnp.int32, (8, 128), 0)
    shifts = [jnp.broadcast_to(g[k : k + 1, :], (8, 128)) for k in range(width)]

    def block(q, _):
        def group(i, acc):
            r = pl.multiple_of(q * 128 + i * 8, 8)
            xs = [
                scores[pl.ds(r, 8), pl.ds(first + 128 * k, 128)] + shifts[k] for k in range(width)
            ]
            peak = jnp.max(functools.reduce(jnp.maximum, xs), axis=1, keepdims=True)
            total = functools.reduce(jnp.add, [jnp.exp2(x - peak) for x in xs])
            value = peak + jnp.log2(jnp.sum(total, axis=1, keepdims=True))
            return jnp.where(lane - i * 8 == sub, value, acc)

        acc = lax.fori_loop(0, 16, group, jnp.zeros((8, 128), F32), unroll=16)
        out[pl.ds(q, 1), :] = jnp.sum(acc, axis=0, keepdims=True)
        return 0

    lax.fori_loop(0, 8, block, 0, unroll=2)


def spread(values, out):
    for q in range(values.shape[0]):
        out[pl.ds(q * 128, 128), :] = jnp.broadcast_to(values[q : q + 1, :], (128, 128)).T


def column_pass(scores, f_rows, out):
    def peaks(i, carry):
        r = pl.multiple_of(i * 8, 8)
        f = f_rows[pl.ds(r, 8), :]
        return tuple(
            jnp.maximum(carry[k], scores[pl.ds(r, 8), pl.ds(128 * k, 128)] + f)
            for k in range(8)
        )

    start = tuple(jnp.full((8, 128), -1e30, F32) for _ in range(8))
    top = lax.fori_loop(0, 128, peaks, start, unroll=16)
    top = [jnp.broadcast_to(jnp.max(t, axis=0, keepdims=True), (8, 128)) for t in top]

    def sums(i, carry):
        r = pl.multiple_of(i * 8, 8)
        f = f_rows[pl.ds(r, 8), :]
        return tuple(
            carry[k] + jnp.exp2(scores[pl.ds(r, 8), pl.ds(128 * k, 128)] + f - top[k])
            for k in range(8)
        )

    start = tuple(jnp.zeros((8, 128), F32) for _ in range(8))
    total = lax.fori_loop(0, 128, sums, start, unroll=16)
    for k in range(8):
        out[k : k + 1, :] = top[k][0:1] + jnp.log2(jnp.sum(total[k], axis=0, keepdims=True))


def kernel(
    source_ref, target_ref, a_ref, b_ref, readout_ref, f_ref, g_ref,
    sources, targets, masses, scores, f_rows, mass_rows, row_buf, column_buf, g_buf, order,
    weights, partial, arrived, arrived_mass,
    own_send, own_recv, far_send, far_recv, y_send, y_recv, in_send, in_recv,
    row_send, row_recv, column_send, column_recv, g_send, g_recv, out_send, out_recv,
):
    at = place()
    x, y, z, c = at
    rows, columns = row_peers(at), column_peers(at)
    barrier = pltpu.get_barrier_semaphore()
    for peer in columns + rows:
        pl.semaphore_signal(barrier, inc=1, device_id=device(*peer), device_id_type=MESH)
    pl.semaphore_wait(barrier, len(columns) + len(rows))

    sibling = (x, y, z, 1 - c)
    own = Gather(targets, pl.ds(0, 1), at, own_send, own_recv)
    far = Gather(targets, pl.ds(1, 3), at, far_send, far_recv)
    own_rows = pl.ds(pl.multiple_of((own.u * 4 + own.v) * 64, 64), 64)
    half_rows = pl.ds(pl.multiple_of(c * 512, 512), 512)
    targets[0, own_rows, :] = target_ref[...]
    own.first()
    own.second(0)
    inner = [
        remote(source_ref, sources.at[half_rows], in_send.at[0], in_recv.at[0], sibling),
        remote(a_ref, masses.at[c], in_send.at[1], in_recv.at[1], sibling),
    ]
    for copy in inner:
        copy.start()
    crossings = []
    for k, step in enumerate((1, 3, 2)):
        dst = targets.at[4 - step, own_rows]
        copy = remote(target_ref, dst, y_send.at[k], y_recv.at[k], (x, (y + step) % 4, z, c))
        copy.start()
        crossings.append(copy)
    sources[half_rows, :] = source_ref[...]
    masses[c] = a_ref[...]

    left = lax.broadcasted_iota(jnp.int32, (8, 128), 1) < 64
    for k in range(16):
        turned = k % 4 * 4 + k // 4
        order[0, k : k + 1, :] = jnp.where(
            c == 0, b_ref[k : k + 1, :], b_ref[turned : turned + 1, :]
        )
    even, odd = order[0, pl.ds(0, 8, stride=2), :], order[0, pl.ds(1, 8, stride=2), :]
    log_b = jnp.log2(
        jnp.where(
            c == 0,
            jnp.where(left, even, pltpu.roll(odd, 64, 1)),
            jnp.where(left, pltpu.roll(even, 64, 1), odd),
        )
    )

    def block_scores(plane, at_column):
        columns_at = pl.ds(at_column, 256)
        product = lax.dot_general(
            sources[...], targets[plane, columns_at, :], NT, preferred_element_type=F32
        )
        scores[plane, :, columns_at] = product * SCALE

    zeros = jnp.zeros((8, 128), F32)

    def own_block(k, du):
        column = own.arrived(du)
        block_scores(0, column)
        row_pass(scores.at[0], zeros, order.at[1 + k], column, 2)

    def far_block(du):
        column = far.arrived(du)
        for plane in (1, 2, 3):
            block_scores(plane, column)

    own.first_forward()
    own.second(3)
    own.second(1)
    own.second_forward(0)
    own.second(2)
    own.second_forward(3)
    own.second_forward(1)
    for copy in inner:
        copy.wait_recv()
    log_a = jnp.log2(jnp.concatenate([masses[0], masses[1]], axis=0))
    own_block(0, 0)
    own.second_forward(2)
    for copy in crossings:
        copy.wait_recv()
    far.first()
    far.second(0)
    own_block(1, 3)
    own_block(2, 1)
    own_block(3, 2)

    def exchange(buf, me, peers, send, recv):
        for peer in peers:
            remote(buf.at[me], buf.at[me], send, recv, peer).start()

    def drain(buf, peers, sem):
        every = buf.at[pl.ds(0, len(peers))]
        pltpu.make_async_copy(every, every, sem).wait()

    def after_row_send(it):
        if it == 0:
            far.first_forward()
        if it == 1:
            far.second_forward(0)
            far.second(2)
        if it == 2:
            far.second_forward(2)
            far_block(3)

    def after_column_send(it):
        if it == 0:
            far.second(3)
            far.second(1)
        if it == 1:
            far.second_forward(3)
            far.second_forward(1)
            far_block(0)
        if it == 2:
            far_block(1)
            far_block(2)

    g = zeros
    row_me, column_me = y * 2 + c, x * 4 + z
    for it in range(ITERS):
        if it == 0:
            row_buf[0, row_me] = combine([order[1 + k, 0:8, :] for k in range(4)])
        else:
            row_pass(scores.at[0], g, row_buf.at[it, row_me])
        exchange(row_buf.at[it], row_me, rows, row_send.at[it], row_recv.at[it])
        after_row_send(it)
        drain(row_buf.at[it], rows, row_recv.at[it])
        lse = combine([row_buf[it, k] for k in range(8)])
        f = log_a - lse
        spread(f, f_rows)
        column_pass(scores.at[0], f_rows, column_buf.at[it, column_me])
        exchange(column_buf.at[it], column_me, columns, column_send.at[it], column_recv.at[it])
        after_column_send(it)
        drain(column_buf.at[it], columns, column_recv.at[it])
        g = log_b - combine([column_buf[it, k] for k in range(16)])

    g_buf[0] = g
    shared = []
    for k, step in enumerate((2, 1, 3)):
        to = (x, (y + step) % 4, z, c)
        shared.append(remote(g_buf.at[0], g_buf.at[4 - step], g_send.at[k], g_recv.at[k], to))
    shared.append(remote(g_buf.at[0], g_buf.at[4], g_send.at[3], g_recv.at[3], sibling))
    for copy in shared:
        copy.start()

    spread(-lse, f_rows)
    mass_rows[...] = jnp.zeros_like(mass_rows)
    other = pl.multiple_of((1 - c) * 512, 512)
    mine = pl.multiple_of(c * 512, 512)

    def weigh(start, plane, slot):
        def group(i, _):
            r = pl.multiple_of(start + i * 16, 16)
            base = f_rows[pl.ds(r, 16), :]
            mass = mass_rows[pl.ds(r, 16), :]
            for q in range(8):
                shift = g_buf[plane, q : q + 1, :]
                w = jnp.exp2(scores[plane, pl.ds(r, 16), pl.ds(q * 128, 128)] + base + shift)
                mass = mass + w
                weights[slot, pl.ds(pl.multiple_of(i * 16, 16), 16), pl.ds(q * 128, 128)] = (
                    w.astype(jnp.bfloat16)
                )
            mass_rows[pl.ds(r, 16), :] = mass
            return 0

        lax.fori_loop(0, 32, group, 0, unroll=8)

    def product(plane, slot):
        return jnp.dot(weights[slot], targets[plane], preferred_element_type=F32)

    weigh(other, 0, 0)
    partial[...] = product(0, 0)
    weigh(mine, 0, 1)
    readout_ref[...] = product(0, 1)
    for copy in shared:
        copy.wait_recv()

    def other_part(plane, _):
        weigh(other, plane, 0)
        partial[...] += product(plane, 0)
        return 0

    lax.fori_loop(1, 4, other_part, 0)
    outward = [
        remote(partial, arrived, out_send.at[0], out_recv.at[0], sibling),
        remote(
            mass_rows.at[pl.ds(other, 512)], arrived_mass, out_send.at[1], out_recv.at[1], sibling
        ),
    ]
    for copy in outward:
        copy.start()

    f_ref[...] = jnp.where(c == 0, f[0:4], f[4:8]) * LN2
    here, there = g_buf[0] * LN2, g_buf[4] * LN2
    g0, g1 = jnp.where(c == 0, here, there), jnp.where(c == 0, there, here)
    order[0, pl.ds(0, 8, stride=2), :] = pltpu.roll(g1, 64, 1)
    order[0, pl.ds(1, 8, stride=2), :] = g1
    order[1, pl.ds(0, 8, stride=2), :] = g0
    order[1, pl.ds(1, 8, stride=2), :] = pltpu.roll(g0, 64, 1)
    for k in range(16):
        turned = k % 4 * 4 + k // 4
        g_ref[k : k + 1, :] = jnp.where(
            left[0:1], order[1, k : k + 1, :], order[0, turned : turned + 1, :]
        )

    def mine_part(plane, _):
        weigh(mine, plane, 1)
        readout_ref[...] += product(plane, 1)
        return 0

    lax.fori_loop(1, 4, mine_part, 0)
    for copy in outward:
        copy.wait_recv()
    mass = mass_rows[pl.ds(mine, 512), :] + arrived_mass[...]
    readout_ref[...] = (readout_ref[...] + arrived[...]) / jnp.sum(mass, axis=1, keepdims=True)

    own.finish()
    far.finish()
    for copy in inner + crossings + shared + outward:
        copy.wait_send()
    for it in range(ITERS):
        drain(row_buf.at[it], rows, row_send.at[it])
        drain(column_buf.at[it], columns, column_send.at[it])


def shards(source_embed, target_embed, source_mass, target_mass):
    vmem, dma = pltpu.VMEM, pltpu.SemaphoreType.DMA
    bf16 = jnp.bfloat16
    readout, f, g = pl.pallas_call(
        kernel,
        out_shape=(
            jax.ShapeDtypeStruct((512, D), F32),
            jax.ShapeDtypeStruct((4, 128), F32),
            jax.ShapeDtypeStruct((16, 128), F32),
        ),
        in_specs=[pl.BlockSpec(memory_space=vmem)] * 4,
        out_specs=(pl.BlockSpec(memory_space=vmem),) * 3,
        scratch_shapes=[
            vmem((1024, D), bf16),
            vmem((4, 1024, D), bf16),
            vmem((2, 4, 128), F32),
            vmem((4, 1024, 1024), F32),
            vmem((1024, 128), F32),
            vmem((1024, 128), F32),
            vmem((ITERS, 8, 8, 128), F32),
            vmem((ITERS, 16, 8, 128), F32),
            vmem((5, 8, 128), F32),
            vmem((5, 16, 128), F32),
            vmem((2, 512, 1024), bf16),
            vmem((512, D), F32),
            vmem((512, D), F32),
            vmem((512, 128), F32),
            dma((5, 6)),
            dma((5, 6)),
            dma((5, 6)),
            dma((5, 6)),
            dma((3,)),
            dma((3,)),
            dma((2,)),
            dma((2,)),
            dma((ITERS,)),
            dma((ITERS,)),
            dma((ITERS,)),
            dma((ITERS,)),
            dma((4,)),
            dma((4,)),
            dma((2,)),
            dma((2,)),
        ],
        name="sinkhorn",
        compiler_params=pltpu.CompilerParams(
            collective_id=0, has_side_effects=True, vmem_limit_bytes=56 << 20
        ),
    )(source_embed, target_embed, source_mass.reshape(4, 128), target_mass.reshape(16, 128))
    return readout, f.reshape(512), g.reshape(2048)


def solution(mesh):
    placed = (P("src", None), P(("tgt", "src"), None), P("src"), P("tgt"))
    return jax.shard_map(
        shards,
        mesh=mesh,
        in_specs=placed,
        out_specs=(P("src", None), P("src"), P("tgt")),
        check_vma=False,
    )
```

time: 114 us -> 78.4 us (0.69)
  Pallas kernels: 109 us -> 73.7 us
    pallas_call x1, Pallas kernels: 109 us -> 73.7 us  [shards(): pl.pallas_call(kernel, out_shape=(jax.ShapeDtypeStruct((512, D), F32), ja...]
where the time goes in v2:
time: 78.4 us; the launch traced here: 78.2 us
  Pallas kernels  73.7 us (94%)
  local copies, waits for them, and re-layouts  3.84 us (5%)
    pallas_call x1, Pallas kernels, shards(): pl.pallas_call(kernel, out_shape=(jax.ShapeDtypeStruct((512, D), F32), ja...  73.7 us
    unnamed x7, local copies, waits for them, and re-layouts  3.84 us

profile of v2, /device:TPU:1, one launch (start us, length us, event | category | flops | bytes accessed | tf_op | source)
XLA Modules:
  0.0 78.2 jit_solution(484435157000178083)
XLA Ops:
  0.6 73.7 %sinkhorn.1 = (f32[512,768]{1,0:T(8,128)}, f32[4,128]{1,0:T(4,128)}, f32[16,128]{1,0:T(8,128)}) custom-call(bf16[512,768]{1,0:T(8,128)(2,1)} %source_ref.1, bf16[64,768]{1,0:T(8,128)(2,1)} %target_ref.1, f32[4,128]{1,0:T(4,128)} %bitcast.6, f32[16,128]{1,0:T(8,128)} %bitcast.4), custom_call_target="tpu_custom_call" | custom-call | tf_op jit(solution)/shard_map/sinkhorn/pallas_call | solution.py:410
  74.4 0.0 copy-start.1
  74.4 0.0 copy-start
  74.4 2.7 %copy.10 = f32[512,768]{1,0:T(8,128)} copy(f32[512,768]{1,0:T(8,128)} %get-tuple-element.12) | data formatting | bytes 3145728
  77.0 0.0 copy-done.1
  77.0 0.6 copy.11
  77.6 0.0 copy-done
  77.6 0.6 copy.12
Async XLA Ops:
  74.4 2.7 %copy-start.1 = (f32[4,128]{1,0:T(4,128)S(1)}, f32[4,128]{1,0:T(4,128)}, u32[]{:S(2)}) copy-start(f32[4,128]{1,0:T(4,128)} %get-tuple-element.7) | copy-start | bytes 6148
  74.4 3.3 %copy-start = (f32[16,128]{1,0:T(8,128)S(1)}, f32[16,128]{1,0:T(8,128)}, u32[]{:S(2)}) copy-start(f32[16,128]{1,0:T(8,128)} %get-tuple-element.8) | copy-start | bytes 24580

commit v3 on v2

--- a/solution.py
+++ b/solution.py
@@ -175,26 +175,36 @@
 
 
 def kernel(
-    source_ref, target_ref, a_ref, b_ref, readout_ref, f_ref, g_ref,
-    sources, targets, masses, scores, f_rows, mass_rows, row_buf, column_buf, g_buf, order,
-    weights, partial, arrived, arrived_mass,
-    own_send, own_recv, far_send, far_recv, y_send, y_recv, in_send, in_recv,
-    row_send, row_recv, column_send, column_recv, g_send, g_recv, out_send, out_recv,
+    source_ref, target_ref, a_ref, b_ref, readout_out, f_out, g_out,
+    readout_ref, f_ref, g_ref,
+    sources, targets, masses, b_buf, scores, f_rows, mass_rows, row_buf, column_buf, g_buf, order,
+    weights_a, weights_b, partial, arrived, arrived_mass,
+    load, own_send, own_recv, far_send, far_recv, y_send, y_recv, in_send, in_recv,
+    row_send, row_recv, column_send, column_recv, g_send, g_recv, out_send, out_recv, store,
 ):
     at = place()
     x, y, z, c = at
     rows, columns = row_peers(at), column_peers(at)
+    own = Gather(targets, pl.ds(0, 1), at, own_send, own_recv)
+    far = Gather(targets, pl.ds(1, 3), at, far_send, far_recv)
+    own_rows = pl.ds(pl.multiple_of((own.u * 4 + own.v) * 64, 64), 64)
+    half_rows = pl.ds(pl.multiple_of(c * 512, 512), 512)
+    own_target = targets.at[0, own_rows]
+    loads = [
+        pltpu.make_async_copy(target_ref, own_target, load.at[0]),
+        pltpu.make_async_copy(a_ref, masses.at[c], load.at[1]),
+        pltpu.make_async_copy(b_ref, b_buf, load.at[2]),
+        pltpu.make_async_copy(source_ref, sources.at[half_rows], load.at[3]),
+    ]
+    for copy in loads:
+        copy.start()
     barrier = pltpu.get_barrier_semaphore()
     for peer in columns + rows:
         pl.semaphore_signal(barrier, inc=1, device_id=device(*peer), device_id_type=MESH)
     pl.semaphore_wait(barrier, len(columns) + len(rows))
 
     sibling = (x, y, z, 1 - c)
-    own = Gather(targets, pl.ds(0, 1), at, own_send, own_recv)
-    far = Gather(targets, pl.ds(1, 3), at, far_send, far_recv)
-    own_rows = pl.ds(pl.multiple_of((own.u * 4 + own.v) * 64, 64), 64)
-    half_rows = pl.ds(pl.multiple_of(c * 512, 512), 512)
-    targets[0, own_rows, :] = target_ref[...]
+    loads[0].wait()
     own.first()
     own.second(0)
     inner = [
@@ -206,17 +216,17 @@
     crossings = []
     for k, step in enumerate((1, 3, 2)):
         dst = targets.at[4 - step, own_rows]
-        copy = remote(target_ref, dst, y_send.at[k], y_recv.at[k], (x, (y + step) % 4, z, c))
+        copy = remote(own_target, dst, y_send.at[k], y_recv.at[k], (x, (y + step) % 4, z, c))
         copy.start()
         crossings.append(copy)
-    sources[half_rows, :] = source_ref[...]
-    masses[c] = a_ref[...]
+    for copy in loads[1:]:
+        copy.wait()
 
     left = lax.broadcasted_iota(jnp.int32, (8, 128), 1) < 64
     for k in range(16):
         turned = k % 4 * 4 + k // 4
         order[0, k : k + 1, :] = jnp.where(
-            c == 0, b_ref[k : k + 1, :], b_ref[turned : turned + 1, :]
+            c == 0, b_buf[k : k + 1, :], b_buf[turned : turned + 1, :]
         )
     even, odd = order[0, pl.ds(0, 8, stride=2), :], order[0, pl.ds(1, 8, stride=2), :]
     log_b = jnp.log2(
@@ -239,7 +249,6 @@
     def own_block(k, du):
         column = own.arrived(du)
         block_scores(0, column)
-        row_pass(scores.at[0], zeros, order.at[1 + k], column, 2)
 
     def far_block(du):
         column = far.arrived(du)
@@ -299,10 +308,7 @@
     g = zeros
     row_me, column_me = y * 2 + c, x * 4 + z
     for it in range(ITERS):
-        if it == 0:
-            row_buf[0, row_me] = combine([order[1 + k, 0:8, :] for k in range(4)])
-        else:
-            row_pass(scores.at[0], g, row_buf.at[it, row_me])
+        row_pass(scores.at[0], g, row_buf.at[it, row_me])
         exchange(row_buf.at[it], row_me, rows, row_send.at[it], row_recv.at[it])
         after_row_send(it)
         drain(row_buf.at[it], rows, row_recv.at[it])
@@ -325,43 +331,41 @@
         copy.start()
 
     spread(-lse, f_rows)
-    mass_rows[...] = jnp.zeros_like(mass_rows)
     other = pl.multiple_of((1 - c) * 512, 512)
     mine = pl.multiple_of(c * 512, 512)
 
-    def weigh(start, plane, slot):
-        def group(i, _):
+    def weigh(start, plane, low):
+        shifts = [g_buf[plane, q : q + 1, :] for q in range(8)]
+        for i in range(32):
             r = pl.multiple_of(start + i * 16, 16)
             base = f_rows[pl.ds(r, 16), :]
-            mass = mass_rows[pl.ds(r, 16), :]
+            parts = [
+                jnp.exp2(scores[plane, pl.ds(r, 16), q * 128 : (q + 1) * 128] + base + shifts[q])
+                for q in range(8)
+            ]
+            mass = functools.reduce(jnp.add, parts)
+            if plane:
+                mass = mass + mass_rows[pl.ds(r, 16), :]
+            mass_rows[pl.ds(r, 16), :] = mass
             for q in range(8):
-                shift = g_buf[plane, q : q + 1, :]
-                w = jnp.exp2(scores[plane, pl.ds(r, 16), pl.ds(q * 128, 128)] + base + shift)
-                mass = mass + w
-                weights[slot, pl.ds(pl.multiple_of(i * 16, 16), 16), pl.ds(q * 128, 128)] = (
-                    w.astype(jnp.bfloat16)
-                )
-            mass_rows[pl.ds(r, 16), :] = mass
-            return 0
-
-        lax.fori_loop(0, 32, group, 0, unroll=8)
-
-    def product(plane, slot):
-        return jnp.dot(weights[slot], targets[plane], preferred_element_type=F32)
-
-    weigh(other, 0, 0)
-    partial[...] = product(0, 0)
-    weigh(mine, 0, 1)
-    readout_ref[...] = product(0, 1)
+                low[i * 16 : (i + 1) * 16, q * 128 : (q + 1) * 128] = parts[q].astype(jnp.bfloat16)
+
+    def product(plane, low, out):
+        value = jnp.dot(low[...], targets[plane], preferred_element_type=F32)
+        out[...] = out[...] + value if plane else value
+
+    weigh(other, 0, weights_a)
+    product(0, weights_a, partial)
+    weigh(mine, 0, weights_b)
     for copy in shared:
         copy.wait_recv()
-
-    def other_part(plane, _):
-        weigh(other, plane, 0)
-        partial[...] += product(plane, 0)
-        return 0
-
-    lax.fori_loop(1, 4, other_part, 0)
+    product(0, weights_b, readout_ref)
+    weigh(other, 1, weights_a)
+    product(1, weights_a, partial)
+    weigh(other, 2, weights_b)
+    product(2, weights_b, partial)
+    weigh(other, 3, weights_a)
+    product(3, weights_a, partial)
     outward = [
         remote(partial, arrived, out_send.at[0], out_recv.at[0], sibling),
         remote(
@@ -384,16 +388,29 @@
             left[0:1], order[1, k : k + 1, :], order[0, turned : turned + 1, :]
         )
 
-    def mine_part(plane, _):
-        weigh(mine, plane, 1)
-        readout_ref[...] += product(plane, 1)
-        return 0
-
-    lax.fori_loop(1, 4, mine_part, 0)
+    weigh(mine, 1, weights_b)
+    product(1, weights_b, readout_ref)
+    weigh(mine, 2, weights_a)
+    product(2, weights_a, readout_ref)
+    weigh(mine, 3, weights_b)
+    product(3, weights_b, readout_ref)
     for copy in outward:
         copy.wait_recv()
-    mass = mass_rows[pl.ds(mine, 512), :] + arrived_mass[...]
-    readout_ref[...] = (readout_ref[...] + arrived[...]) / jnp.sum(mass, axis=1, keepdims=True)
+    stores = [
+        pltpu.make_async_copy(f_ref, f_out, store.at[4]),
+        pltpu.make_async_copy(g_ref, g_out, store.at[5]),
+    ]
+    for copy in stores:
+        copy.start()
+    for k in range(4):
+        part = pl.ds(k * 128, 128)
+        mass = mass_rows[pl.ds(pl.multiple_of(mine + k * 128, 128), 128), :] + arrived_mass[part, :]
+        readout_ref[part, :] = (readout_ref[part, :] + arrived[part, :]) * (
+            1.0 / jnp.sum(mass, axis=1, keepdims=True)
+        )
+        copy = pltpu.make_async_copy(readout_ref.at[part], readout_out.at[part], store.at[k])
+        copy.start()
+        stores.append(copy)
 
     own.finish()
     far.finish()
@@ -402,6 +419,24 @@
     for it in range(ITERS):
         drain(row_buf.at[it], rows, row_send.at[it])
         drain(column_buf.at[it], columns, column_send.at[it])
+    for copy in stores:
+        copy.wait()
+
+
+def finish(readout, f, g, readout_out, f_out, g_out, held, held_f, held_g, load, store):
+    pairs = [(f, held_f, f_out), (g, held_g, g_out)]
+    for k in range(8):
+        part = pl.ds(k * 64, 64)
+        pairs.append((readout.at[part], held.at[part], readout_out.at[part]))
+    loads = [pltpu.make_async_copy(a, b, load.at[k]) for k, (a, b, _) in enumerate(pairs)]
+    stores = [pltpu.make_async_copy(b, o, store.at[k]) for k, (_, b, o) in enumerate(pairs)]
+    for copy in loads:
+        copy.start()
+    for before, after in zip(loads, stores):
+        before.wait()
+        after.start()
+    for copy in stores:
+        copy.wait()
 
 
 def shards(source_embed, target_embed, source_mass, target_mass):
@@ -414,12 +449,16 @@
             jax.ShapeDtypeStruct((4, 128), F32),
             jax.ShapeDtypeStruct((16, 128), F32),
         ),
-        in_specs=[pl.BlockSpec(memory_space=vmem)] * 4,
-        out_specs=(pl.BlockSpec(memory_space=vmem),) * 3,
+        in_specs=[pl.BlockSpec(memory_space=pltpu.HBM)] * 4,
+        out_specs=(pl.BlockSpec(memory_space=pltpu.HBM),) * 3,
         scratch_shapes=[
+            vmem((512, D), F32),
+            vmem((4, 128), F32),
+            vmem((16, 128), F32),
             vmem((1024, D), bf16),
             vmem((4, 1024, D), bf16),
             vmem((2, 4, 128), F32),
+            vmem((16, 128), F32),
             vmem((4, 1024, 1024), F32),
             vmem((1024, 128), F32),
             vmem((1024, 128), F32),
@@ -427,10 +466,12 @@
             vmem((ITERS, 16, 8, 128), F32),
             vmem((5, 8, 128), F32),
             vmem((5, 16, 128), F32),
-            vmem((2, 512, 1024), bf16),
+            vmem((512, 1024), bf16),
+            vmem((512, 1024), bf16),
             vmem((512, D), F32),
             vmem((512, D), F32),
             vmem((512, 128), F32),
+            dma((4,)),
             dma((5, 6)),
             dma((5, 6)),
             dma((5, 6)),
@@ -447,12 +488,32 @@
             dma((4,)),
             dma((2,)),
             dma((2,)),
+            dma((6,)),
         ],
         name="sinkhorn",
         compiler_params=pltpu.CompilerParams(
             collective_id=0, has_side_effects=True, vmem_limit_bytes=56 << 20
         ),
     )(source_embed, target_embed, source_mass.reshape(4, 128), target_mass.reshape(16, 128))
+    readout, f, g = pl.pallas_call(
+        finish,
+        out_shape=(
+            jax.ShapeDtypeStruct((512, D), F32),
+            jax.ShapeDtypeStruct((4, 128), F32),
+            jax.ShapeDtypeStruct((16, 128), F32),
+        ),
+        in_specs=[pl.BlockSpec(memory_space=pl.ANY)] * 3,
+        out_specs=(pl.BlockSpec(memory_space=pl.ANY),) * 3,
+        scratch_shapes=[
+            vmem((512, D), F32),
+            vmem((4, 128), F32),
+            vmem((16, 128), F32),
+            dma((10,)),
+            dma((10,)),
+        ],
+        name="finish",
+        compiler_params=pltpu.CompilerParams(vmem_limit_bytes=60 << 20),
+    )(readout, f, g)
     return readout, f.reshape(512), g.reshape(2048)
 
 

time: 78.4 us -> 74.7 us (0.953)
  local copies, waits for them, and re-layouts: 3.84 us -> 0 us
    unnamed x7 -> x0, local copies, waits for them, and re-layouts: 3.84 us -> none
    pallas_call x0 -> x1, Pallas kernels: none -> 2.35 us  [shards(): pl.pallas_call(finish, out_shape=(jax.ShapeDtypeStruct((512, D), F32), ja...]
    pallas_call x1, Pallas kernels: 73.7 us -> 71.5 us  [shards(): pl.pallas_call(kernel, out_shape=(jax.ShapeDtypeStruct((512, D), F32), ja...]
where the time goes in v3:
time: 74.7 us; the launch traced here: 74.6 us
  Pallas kernels  73.8 us (99%)
  between operations  0.8 us (1%)
    pallas_call x1, Pallas kernels, shards(): pl.pallas_call(kernel, out_shape=(jax.ShapeDtypeStruct((512, D), F32), ja...  71.5 us
    pallas_call x1, Pallas kernels, shards(): pl.pallas_call(finish, out_shape=(jax.ShapeDtypeStruct((512, D), F32), ja...  2.35 us

profile of v3, /device:TPU:1, one launch (start us, length us, event | category | flops | bytes accessed | tf_op | source)
XLA Modules:
  0.0 74.6 jit_solution(9149850839555929086)
XLA Ops:
  0.6 71.5 %sinkhorn.1 = (f32[512,768]{1,0:T(8,128)}, f32[4,128]{1,0:T(4,128)}, f32[16,128]{1,0:T(8,128)}) custom-call(bf16[512,768]{1,0:T(8,128)(2,1)} %source_ref.1, bf16[64,768]{1,0:T(8,128)(2,1)} %target_ref.1, f32[4,128]{1,0:T(4,128)} %bitcast.5, f32[16,128]{1,0:T(8,128)} %bitcast.4), custom_call_target="tpu_custom_call" | custom-call | tf_op jit(solution)/shard_map/sinkhorn/pallas_call | solution.py:445
  72.1 2.3 %finish.1 = (f32[512,768]{1,0:T(8,128)}, f32[4,128]{1,0:T(4,128)}, f32[16,128]{1,0:T(8,128)}) custom-call(f32[512,768]{1,0:T(8,128)} %get-tuple-element.9.readout, f32[4,128]{1,0:T(4,128)} %get-tuple-element.10.f, f32[16,128]{1,0:T(8,128)} %get-tuple-element.11.g), custom_call_target="tpu_custom_call" | custom-call | tf_op jit(solution)/shard_map/finish/pallas_call | solution.py:498

commit v4 on v3

--- a/solution.py
+++ b/solution.py
@@ -119,17 +119,15 @@
     return peak + jnp.log2(functools.reduce(jnp.add, [jnp.exp2(p - peak) for p in parts]))
 
 
-def row_pass(scores, g, out, first=0, width=8):
+def row_pass(scores, g, half, out):
     lane = lax.broadcasted_iota(jnp.int32, (8, 128), 1)
     sub = lax.broadcasted_iota(jnp.int32, (8, 128), 0)
-    shifts = [jnp.broadcast_to(g[k : k + 1, :], (8, 128)) for k in range(width)]
+    shifts = [jnp.broadcast_to(g[k : k + 1, :], (8, 128)) for k in range(8)]
 
     def block(q, _):
         def group(i, acc):
-            r = pl.multiple_of(q * 128 + i * 8, 8)
-            xs = [
-                scores[pl.ds(r, 8), pl.ds(first + 128 * k, 128)] + shifts[k] for k in range(width)
-            ]
+            r = pl.multiple_of(half * 512 + q * 128 + i * 8, 8)
+            xs = [scores[pl.ds(r, 8), pl.ds(128 * k, 128)] + shifts[k] for k in range(8)]
             peak = jnp.max(functools.reduce(jnp.maximum, xs), axis=1, keepdims=True)
             total = functools.reduce(jnp.add, [jnp.exp2(x - peak) for x in xs])
             value = peak + jnp.log2(jnp.sum(total, axis=1, keepdims=True))
@@ -139,17 +137,18 @@
         out[pl.ds(q, 1), :] = jnp.sum(acc, axis=0, keepdims=True)
         return 0
 
-    lax.fori_loop(0, 8, block, 0, unroll=2)
-
-
-def spread(values, out):
+    lax.fori_loop(0, 4, block, 0, unroll=2)
+
+
+def spread(values, out, first=0):
     for q in range(values.shape[0]):
-        out[pl.ds(q * 128, 128), :] = jnp.broadcast_to(values[q : q + 1, :], (128, 128)).T
-
-
-def column_pass(scores, f_rows, out):
+        rows = pl.ds(first + q * 128, 128)
+        out[rows, :] = jnp.broadcast_to(values[q : q + 1, :], (128, 128)).T
+
+
+def column_half(scores, f_rows, half):
     def peaks(i, carry):
-        r = pl.multiple_of(i * 8, 8)
+        r = pl.multiple_of(half * 512 + i * 8, 8)
         f = f_rows[pl.ds(r, 8), :]
         return tuple(
             jnp.maximum(carry[k], scores[pl.ds(r, 8), pl.ds(128 * k, 128)] + f)
@@ -157,11 +156,11 @@
         )
 
     start = tuple(jnp.full((8, 128), -1e30, F32) for _ in range(8))
-    top = lax.fori_loop(0, 128, peaks, start, unroll=16)
+    top = lax.fori_loop(0, 64, peaks, start, unroll=16)
     top = [jnp.broadcast_to(jnp.max(t, axis=0, keepdims=True), (8, 128)) for t in top]
 
     def sums(i, carry):
-        r = pl.multiple_of(i * 8, 8)
+        r = pl.multiple_of(half * 512 + i * 8, 8)
         f = f_rows[pl.ds(r, 8), :]
         return tuple(
             carry[k] + jnp.exp2(scores[pl.ds(r, 8), pl.ds(128 * k, 128)] + f - top[k])
@@ -169,9 +168,15 @@
         )
 
     start = tuple(jnp.zeros((8, 128), F32) for _ in range(8))
-    total = lax.fori_loop(0, 128, sums, start, unroll=16)
+    return top, lax.fori_loop(0, 64, sums, start, unroll=16)
+
+
+def join_columns(first, second, out):
     for k in range(8):
-        out[k : k + 1, :] = top[k][0:1] + jnp.log2(jnp.sum(total[k], axis=0, keepdims=True))
+        peak = jnp.maximum(first[0][k], second[0][k])
+        total = first[1][k] * jnp.exp2(first[0][k] - peak)
+        total = total + second[1][k] * jnp.exp2(second[0][k] - peak)
+        out[k : k + 1, :] = peak[0:1] + jnp.log2(jnp.sum(total, axis=0, keepdims=True))
 
 
 def kernel(
@@ -252,8 +257,12 @@
 
     def far_block(du):
         column = far.arrived(du)
-        for plane in (1, 2, 3):
+
+        def one(plane, _):
             block_scores(plane, column)
+            return 0
+
+        lax.fori_loop(1, 4, one, 0)
 
     own.first_forward()
     own.second(3)
@@ -308,14 +317,19 @@
     g = zeros
     row_me, column_me = y * 2 + c, x * 4 + z
     for it in range(ITERS):
-        row_pass(scores.at[0], g, row_buf.at[it, row_me])
-        exchange(row_buf.at[it], row_me, rows, row_send.at[it], row_recv.at[it])
+        for h in (0, 1):
+            row_pass(scores.at[0], g, h, row_buf.at[it, h, row_me])
+            exchange(row_buf.at[it, h], row_me, rows, row_send.at[it, h], row_recv.at[it, h])
         after_row_send(it)
-        drain(row_buf.at[it], rows, row_recv.at[it])
-        lse = combine([row_buf[it, k] for k in range(8)])
-        f = log_a - lse
-        spread(f, f_rows)
-        column_pass(scores.at[0], f_rows, column_buf.at[it, column_me])
+        halves, lses, fs = [], [], []
+        for h in (0, 1):
+            drain(row_buf.at[it, h], rows, row_recv.at[it, h])
+            lses.append(combine([row_buf[it, h, k] for k in range(8)]))
+            fs.append(log_a[h * 4 : h * 4 + 4] - lses[h])
+            spread(fs[h], f_rows, h * 512)
+            halves.append(column_half(scores.at[0], f_rows, h))
+        lse, f = jnp.concatenate(lses, axis=0), jnp.concatenate(fs, axis=0)
+        join_columns(*halves, column_buf.at[it, column_me])
         exchange(column_buf.at[it], column_me, columns, column_send.at[it], column_recv.at[it])
         after_column_send(it)
         drain(column_buf.at[it], columns, column_recv.at[it])
@@ -417,7 +431,8 @@
     for copy in inner + crossings + shared + outward:
         copy.wait_send()
     for it in range(ITERS):
-        drain(row_buf.at[it], rows, row_send.at[it])
+        for h in (0, 1):
+            drain(row_buf.at[it, h], rows, row_send.at[it, h])
         drain(column_buf.at[it], columns, column_send.at[it])
     for copy in stores:
         copy.wait()
@@ -462,7 +477,7 @@
             vmem((4, 1024, 1024), F32),
             vmem((1024, 128), F32),
             vmem((1024, 128), F32),
-            vmem((ITERS, 8, 8, 128), F32),
+            vmem((ITERS, 2, 8, 4, 128), F32),
             vmem((ITERS, 16, 8, 128), F32),
             vmem((5, 8, 128), F32),
             vmem((5, 16, 128), F32),
@@ -480,8 +495,8 @@
             dma((3,)),
             dma((2,)),
             dma((2,)),
-            dma((ITERS,)),
-            dma((ITERS,)),
+            dma((ITERS, 2)),
+            dma((ITERS, 2)),
             dma((ITERS,)),
             dma((ITERS,)),
             dma((4,)),

time: 74.7 us -> 73.4 us (0.983)
  Pallas kernels: 73.8 us -> 72.4 us
    pallas_call x1, Pallas kernels: 71.5 us -> 70.1 us  [shards(): pl.pallas_call(kernel, out_shape=(jax.ShapeDtypeStruct((512, D), F32), ja...]
where the time goes in v4:
time: 73.4 us; the launch traced here: 73.2 us
  Pallas kernels  72.4 us (99%)
  between operations  0.8 us (1%)
    pallas_call x1, Pallas kernels, shards(): pl.pallas_call(kernel, out_shape=(jax.ShapeDtypeStruct((512, D), F32), ja...  70.1 us
    pallas_call x1, Pallas kernels, shards(): pl.pallas_call(finish, out_shape=(jax.ShapeDtypeStruct((512, D), F32), ja...  2.35 us

profile of v4, /device:TPU:1, one launch (start us, length us, event | category | flops | bytes accessed | tf_op | source)
XLA Modules:
  0.0 73.2 jit_solution(1917553622325975695)
XLA Ops:
  0.6 70.1 %sinkhorn.1 = (f32[512,768]{1,0:T(8,128)}, f32[4,128]{1,0:T(4,128)}, f32[16,128]{1,0:T(8,128)}) custom-call(bf16[512,768]{1,0:T(8,128)(2,1)} %source_ref.1, bf16[64,768]{1,0:T(8,128)(2,1)} %target_ref.1, f32[4,128]{1,0:T(4,128)} %bitcast.5, f32[16,128]{1,0:T(8,128)} %bitcast.4), custom_call_target="tpu_custom_call" | custom-call | tf_op jit(solution)/shard_map/sinkhorn/pallas_call | solution.py:460
  70.7 2.3 %finish.1 = (f32[512,768]{1,0:T(8,128)}, f32[4,128]{1,0:T(4,128)}, f32[16,128]{1,0:T(8,128)}) custom-call(f32[512,768]{1,0:T(8,128)} %get-tuple-element.9.readout, f32[4,128]{1,0:T(4,128)} %get-tuple-element.10.f, f32[16,128]{1,0:T(8,128)} %get-tuple-element.11.g), custom_call_target="tpu_custom_call" | custom-call | tf_op jit(solution)/shard_map/finish/pallas_call | solution.py:513

commit v5 on v4

--- a/solution.py
+++ b/solution.py
@@ -278,11 +278,11 @@
     own.second_forward(2)
     for copy in crossings:
         copy.wait_recv()
+    own_block(1, 3)
     far.first()
-    far.second(0)
-    own_block(1, 3)
     own_block(2, 1)
     own_block(3, 2)
+    far.second(0)
 
     def exchange(buf, me, peers, send, recv):
         for peer in peers:
@@ -292,12 +292,21 @@
         every = buf.at[pl.ds(0, len(peers))]
         pltpu.make_async_copy(every, every, sem).wait()
 
+    def sent(it):
+        for h in (0, 1):
+            drain(row_buf.at[it, h], rows, row_send.at[it, h])
+        drain(column_buf.at[it], columns, column_send.at[it])
+
     def after_row_send(it):
+        if it == 1:
+            own.finish()
+            for copy in inner + crossings:
+                copy.wait_send()
+            sent(0)
         if it == 0:
             far.first_forward()
         if it == 1:
             far.second_forward(0)
-            far.second(2)
         if it == 2:
             far.second_forward(2)
             far_block(3)
@@ -308,6 +317,7 @@
             far.second(1)
         if it == 1:
             far.second_forward(3)
+            far.second(2)
             far.second_forward(1)
             far_block(0)
         if it == 2:
@@ -371,6 +381,9 @@
     weigh(other, 0, weights_a)
     product(0, weights_a, partial)
     weigh(mine, 0, weights_b)
+    for it in (1, 2):
+        sent(it)
+    far.finish()
     for copy in shared:
         copy.wait_recv()
     product(0, weights_b, readout_ref)
@@ -426,14 +439,8 @@
         copy.start()
         stores.append(copy)
 
-    own.finish()
-    far.finish()
-    for copy in inner + crossings + shared + outward:
+    for copy in shared + outward:
         copy.wait_send()
-    for it in range(ITERS):
-        for h in (0, 1):
-            drain(row_buf.at[it, h], rows, row_send.at[it, h])
-        drain(column_buf.at[it], columns, column_send.at[it])
     for copy in stores:
         copy.wait()
 

time: 73.4 us -> 73.2 us (level)
  no operation moved by 1% of the time
where the time goes in v5:
time: 73.2 us; the launch traced here: 73 us
  Pallas kernels  72.2 us (99%)
  between operations  0.8 us (1%)
    pallas_call x1, Pallas kernels, shards(): pl.pallas_call(kernel, out_shape=(jax.ShapeDtypeStruct((512, D), F32), ja...  69.9 us
    pallas_call x1, Pallas kernels, shards(): pl.pallas_call(finish, out_shape=(jax.ShapeDtypeStruct((512, D), F32), ja...  2.35 us

profile of v5, /device:TPU:1, one launch (start us, length us, event | category | flops | bytes accessed | tf_op | source)
XLA Modules:
  0.0 73.0 jit_solution(12971407619195695115)
XLA Ops:
  0.6 69.9 %sinkhorn.1 = (f32[512,768]{1,0:T(8,128)}, f32[4,128]{1,0:T(4,128)}, f32[16,128]{1,0:T(8,128)}) custom-call(bf16[512,768]{1,0:T(8,128)(2,1)} %source_ref.1, bf16[64,768]{1,0:T(8,128)(2,1)} %target_ref.1, f32[4,128]{1,0:T(4,128)} %bitcast.5, f32[16,128]{1,0:T(8,128)} %bitcast.4), custom_call_target="tpu_custom_call" | custom-call | tf_op jit(solution)/shard_map/sinkhorn/pallas_call | solution.py:467
  70.5 2.3 %finish.1 = (f32[512,768]{1,0:T(8,128)}, f32[4,128]{1,0:T(4,128)}, f32[16,128]{1,0:T(8,128)}) custom-call(f32[512,768]{1,0:T(8,128)} %get-tuple-element.9.readout, f32[4,128]{1,0:T(4,128)} %get-tuple-element.10.f, f32[16,128]{1,0:T(8,128)} %get-tuple-element.11.g), custom_call_target="tpu_custom_call" | custom-call | tf_op jit(solution)/shard_map/finish/pallas_call | solution.py:520

commit v6 on v5

--- a/solution.py
+++ b/solution.py
@@ -137,7 +137,7 @@
         out[pl.ds(q, 1), :] = jnp.sum(acc, axis=0, keepdims=True)
         return 0
 
-    lax.fori_loop(0, 4, block, 0, unroll=2)
+    lax.fori_loop(0, 4, block, 0, unroll=4)
 
 
 def spread(values, out, first=0):
@@ -156,7 +156,7 @@
         )
 
     start = tuple(jnp.full((8, 128), -1e30, F32) for _ in range(8))
-    top = lax.fori_loop(0, 64, peaks, start, unroll=16)
+    top = lax.fori_loop(0, 64, peaks, start, unroll=64)
     top = [jnp.broadcast_to(jnp.max(t, axis=0, keepdims=True), (8, 128)) for t in top]
 
     def sums(i, carry):
@@ -168,7 +168,7 @@
         )
 
     start = tuple(jnp.zeros((8, 128), F32) for _ in range(8))
-    return top, lax.fori_loop(0, 64, sums, start, unroll=16)
+    return top, lax.fori_loop(0, 64, sums, start, unroll=64)
 
 
 def join_columns(first, second, out):

time: 73.2 us -> 73 us (level)
  no operation moved by 1% of the time
where the time goes in v6:
time: 73 us; the launch traced here: 72.9 us
  Pallas kernels  72.1 us (99%)
  between operations  0.8 us (1%)
    pallas_call x1, Pallas kernels, shards(): pl.pallas_call(kernel, out_shape=(jax.ShapeDtypeStruct((512, D), F32), ja...  69.7 us
    pallas_call x1, Pallas kernels, shards(): pl.pallas_call(finish, out_shape=(jax.ShapeDtypeStruct((512, D), F32), ja...  2.35 us

profile of v6, /device:TPU:1, one launch (start us, length us, event | category | flops | bytes accessed | tf_op | source)
XLA Modules:
  0.0 72.9 jit_solution(7546960197829317496)
XLA Ops:
  0.6 69.7 %sinkhorn.1 = (f32[512,768]{1,0:T(8,128)}, f32[4,128]{1,0:T(4,128)}, f32[16,128]{1,0:T(8,128)}) custom-call(bf16[512,768]{1,0:T(8,128)(2,1)} %source_ref.1, bf16[64,768]{1,0:T(8,128)(2,1)} %target_ref.1, f32[4,128]{1,0:T(4,128)} %bitcast.5, f32[16,128]{1,0:T(8,128)} %bitcast.4), custom_call_target="tpu_custom_call" | custom-call | tf_op jit(solution)/shard_map/sinkhorn/pallas_call | solution.py:467
  70.4 2.3 %finish.1 = (f32[512,768]{1,0:T(8,128)}, f32[4,128]{1,0:T(4,128)}, f32[16,128]{1,0:T(8,128)}) custom-call(f32[512,768]{1,0:T(8,128)} %get-tuple-element.9.readout, f32[4,128]{1,0:T(4,128)} %get-tuple-element.10.f, f32[16,128]{1,0:T(8,128)} %get-tuple-element.11.g), custom_call_target="tpu_custom_call" | custom-call | tf_op jit(solution)/shard_map/finish/pallas_call | solution.py:520
